TPU v7x, 512 devices: a whole 4x8x8 slice. The times are simulated.
512 devices in a mesh: grp: 4 (over y_hi), seq: 16 (over z, core), voc: 8 (over x, y_lo).
Axes of the slice: x: 4, y: 8 (y_hi: 4, y_lo: 2; y = y_hi * 2 + y_lo), z: 8, core: 2. Of those that a mesh axis runs over, the one named last changes fastest.
Arguments:
- residual: bfloat16 [1536, 12288], P(('grp', 'voc'), 'seq'), may hold values from -36 to 36
- norm_gain: float32 [12288], P('seq'), may hold values from 0.5 to 1.5
- head_weight: bfloat16 [16384, 12288], P(('grp', 'voc'), 'seq'), may hold values from -1 to 1
- actions: int32 [1536], replicated, may hold values from 0 to 16383
- behavior_logp: float32 [1536], replicated, may hold values from -30 to -14
- advantages: float32 [1536], replicated, may hold values from -4 to 4
- decision_mask: int32 [1536], replicated, may hold values 0 or 1
- clip_tenths: int32 [1536], replicated, may hold values from 5 to 20
Outputs:
- loss: float32 [], replicated
- head_grad: bfloat16 [16384, 12288], P(('grp', 'voc'), 'seq')
- hidden_grad: float32 [1536, 12288], P(('grp', 'voc'), 'seq')
All inputs are finite; a program needn't handle non-finite values.
Results may differ from a plain program's by a relative error of at most 0.01875.
Values may be sent and summed in bfloat16 or wider, within the bound.
A program may use at most 64 MiB of HBM per device.

v0:
```python
import jax
import jax.numpy as jnp
from jax import lax
from jax.sharding import PartitionSpec as P

D = 12288


EPSILON = 1e-05
GRAD_SCALE = 8.0


def head_terms(logits, actions, behavior_logp, advantages, decision_mask, clip_tenths):
    col_count = logits.shape[1]
    taken = actions - lax.axis_index(("grp", "voc")) * col_count
    is_taken = jnp.arange(col_count, dtype=jnp.int32)[None, :] == taken[:, None]
    picked_here = jnp.sum(jnp.where(is_taken, logits, 0.0), axis=1)
    row_top = lax.pmax(jnp.max(logits, axis=1), ("grp", "voc"))
    exp_total, picked = lax.psum(
        (jnp.sum(jnp.exp(logits - row_top[:, None]), axis=1), picked_here), ("grp", "voc")
    )
    log_norm = row_top + jnp.log(exp_total)
    log_prob = picked - log_norm
    trunc_level = clip_tenths.astype(jnp.float32) / 10.0
    decisions = decision_mask.astype(jnp.float32)
    ratio_weight = jnp.minimum(jnp.exp(log_prob - behavior_logp), trunc_level)
    scaled = decisions * ratio_weight * advantages
    loss_part = jnp.sum(scaled * log_prob)
    softmax = jnp.exp(logits - log_norm[:, None])
    dlogits = ((GRAD_SCALE * scaled)[:, None] * (softmax - is_taken.astype(jnp.float32))).astype(
        jnp.bfloat16
    )
    return (dlogits, loss_part)


def per_device(
    residual, norm_gain, head_weight, actions, behavior_logp, advantages, decision_mask, clip_tenths
):
    token_count = actions.shape[0]
    own_rows = residual.astype(jnp.float32)
    squares = lax.psum(jnp.sum(own_rows * own_rows, axis=1), "seq")
    inv_rms = lax.rsqrt(squares / D + EPSILON)
    hidden = (own_rows * inv_rms[:, None] * norm_gain[None, :]).astype(jnp.bfloat16)
    hidden_all = lax.all_gather(hidden, ("grp", "voc"), axis=0, tiled=True)
    logit_part = jnp.einsum(
        "td,vd->tv", hidden_all, head_weight, preferred_element_type=jnp.float32
    )
    logits = lax.psum(logit_part, "seq")
    dlogits_all, loss_part = head_terms(
        logits, actions, behavior_logp, advantages, decision_mask, clip_tenths
    )
    loss = -loss_part / token_count
    head_grad = jnp.einsum(
        "tv,td->vd", dlogits_all, hidden_all, preferred_element_type=jnp.float32
    ).astype(jnp.bfloat16)
    hidden_grad = lax.psum_scatter(
        jnp.dot(dlogits_all, head_weight, preferred_element_type=jnp.float32).astype(jnp.bfloat16),
        ("grp", "voc"),
        scatter_dimension=0,
        tiled=True,
    ).astype(jnp.float32)
    return (loss, head_grad, hidden_grad)


def solution(mesh):
    in_specs = (
        P(("grp", "voc"), "seq"),
        P("seq"),
        P(("grp", "voc"), "seq"),
        P(),
        P(),
        P(),
        P(),
        P(),
    )
    out_specs = (P(), P(("grp", "voc"), "seq"), P(("grp", "voc"), "seq"))
    return jax.shard_map(
        per_device, mesh=mesh, in_specs=in_specs, out_specs=out_specs, check_vma=False
    )
```

profile of v0, /device:TPU:64, one launch (start us, length us, event | category | flops | bytes accessed | tf_op | source)
XLA Modules:
  0.0 695.2 jit_solution(16707033085550951406)
XLA Ops:
  7.2 0.0 copy-start
  7.2 0.0 all-gather.2.cloned.1.call-start
  7.2 1.1 fusion
  8.3 28.2 %psum.28 = f32[48]{0:T(128)S(1)} all-reduce(f32[48]{0:T(128)S(1)} %fusion), channel_id=1, replica_groups=mesh['grp'=4,'seq'=16,'voc'=8] {'seq'}, use_global_device_ids=true, to_apply=%region_1.0 | all-reduce | flops 48 | bytes 384 | tf_op jit(solution)/shard_map/psum | solution.py:41
  36.5 1.6 fusion.2
  38.1 0.0 all-gather.2.cloned.1.call-update
  38.1 0.0 all-reduce.3.cloned.1.call-start
  38.2 147.0 %all-gather.2.cloned.1.call-done = bf16[1536,768]{1,0:T(8,128)(2,1)} async-done(((bf16[48,768]{1,0:T(8,128)(2,1)}), bf16[1536,768]{1,0:T(8,128)(2,1)}) %all-gather.2.cloned.1.call-update) | async-done | bytes 2359312 | tf_op jit(solution)/shard_map/all_gather | solution.py:44
  185.2 4.8 fusion.3
  189.9 0.0 all-reduce.3.cloned.1.call-update
  190.0 0.0 reduce-scatter.2.cloned.1.call-start
  190.0 0.6 copy-done.5
  190.7 118.4 %all-reduce.3.cloned.1.call-done = f32[1536,512]{1,0:T(8,128)} async-done(((f32[1536,512]{1,0:T(8,128)}), f32[1536,512]{1,0:T(8,128)}) %all-reduce.3.cloned.1.call-update) | async-done | bytes 3145744 | tf_op jit(solution)/shard_map/psum | solution.py:48
  309.1 2.2 reduce_max.9
  311.3 75.6 %pmax.7 = f32[1536]{0:T(1024)S(1)} all-reduce(f32[1536]{0:T(1024)S(1)} %reduce_max.9), channel_id=1, replica_groups=mesh['grp'=4,'seq'=16,'voc'=8] {'grp','voc'}, use_global_device_ids=true, to_apply=%region_6.7 | all-reduce | flops 1536 | bytes 12288 | tf_op jit(solution)/shard_map/pmax | solution.py:18
  386.9 3.0 exponential_reduce_fusion
  389.8 137.7 %all-reduce = (f32[1536]{0:T(1024)S(1)}, f32[1536]{0:T(1024)S(1)}) all-reduce(f32[1536]{0:T(1024)S(1)} %get-tuple-element.4, f32[1536]{0:T(1024)S(1)} %get-tuple-element.3), channel_id=1, replica_groups=mesh['grp'=4,'seq'=16,'voc'=8] {'grp','voc'}, use_global_device_ids=true, to_apply=%region_4.5 | all-reduce | flops 3072 | bytes 24576 | tf_op jit(solution)/shard_map/psum | solution.py:19
  527.6 2.7 multiply_convert_fusion
  530.2 2.8 convolution_convert_fusion
  533.0 0.0 reduce-scatter.2.cloned.1.call-update
  533.1 0.6 multiply_reduce_fusion
  534.3 4.0 convolution_convert_fusion.1
  538.3 147.6 %reduce-scatter.2.cloned.1.call-done = bf16[48,768]{1,0:T(8,128)(2,1)} async-done(((bf16[1536,768]{1,0:T(8,128)(2,1)}), bf16[48,768]{1,0:T(8,128)(2,1)}) %reduce-scatter.2.cloned.1.call-update) | async-done | bytes 73744 | tf_op jit(solution)/shard_map/reduce_scatter | solution.py:56
  685.9 1.6 convert_element_type.35
  (13 shorter events, 0.1 us)
Async XLA Ops:
  7.2 178.0 %copy-start = (bf16[512,768]{1,0:T(8,128)(2,1)S(1)}, bf16[512,768]{1,0:T(8,128)(2,1)}, u32[]{:S(2)}) copy-start(bf16[512,768]{1,0:T(8,128)(2,1)} %param.10) | copy-start | bytes 2359300
  7.2 178.0 %all-gather.2.cloned.1.call-start = ((), (), s32[]{:S(2)}) async-start(), calls=%async_computation.1 | async-start | bytes 2433024 | tf_op jit(solution)/shard_map/all_gather | solution.py:44
  38.1 271.0 %all-reduce.3.cloned.1.call-start = ((), (), s32[]{:S(2)}) async-start(), calls=%async_computation.2 | async-start | bytes 6291456 | tf_op jit(solution)/shard_map/psum | solution.py:48
  189.9 0.7 copy-start.5
  190.0 496.0 %reduce-scatter.2.cloned.1.call-start = ((), (), s32[]{:S(2)}) async-start(), calls=%async_computation.3 | async-start | bytes 2433024 | tf_op jit(solution)/shard_map/reduce_scatter | solution.py:56
  190.6 336.9 %copy-start.1 = (f32[1536]{0:T(1024)S(1)}, f32[1536]{0:T(1024)}, u32[]{:S(2)}) copy-start(f32[1536]{0:T(1024)} %param.13) | copy-start | bytes 18436
  190.6 336.9 %copy-start.2 = (s32[1536]{0:T(1024)S(1)}, s32[1536]{0:T(1024)}, u32[]{:S(2)}) copy-start(s32[1536]{0:T(1024)} %param.15) | copy-start | bytes 18436
  190.7 336.9 %copy-start.3 = (f32[1536]{0:T(1024)S(1)}, f32[1536]{0:T(1024)}, u32[]{:S(2)}) copy-start(f32[1536]{0:T(1024)} %param.12) | copy-start | bytes 18436
  190.7 336.9 %copy-start.4 = (s32[1536]{0:T(1024)S(1)}, s32[1536]{0:T(1024)}, u32[]{:S(2)}) copy-start(s32[1536]{0:T(1024)} %param.14) | copy-start | bytes 18436
Sparse Core Ops, SparseCore 0:
  38.2 146.8 all-gather.1
  190.1 118.9 all-reduce.2
  533.2 152.7 reduce-scatter.1
where the time goes:
time: 696 us; the launch traced here: 695 us
  waiting for transfers between devices  413 us (59%)
  blocking collectives  241 us (35%)
  between operations  15.6 us (2%)
  other arithmetic  12.6 us (2%)
  matrix products  11.6 us (2%)
    reduce_scatter x1, waiting for transfers between devices, per_device(): lax.psum_scatter(jnp.dot(dlogits_all, head_weight, preferred_element_type...  148 us
    all_gather x1, waiting for transfers between devices, per_device(): hidden_all = lax.all_gather(hidden, ('grp', 'voc'), axis=0, tiled=True)  147 us
    psum x1, blocking collectives, head_terms(): lax.psum((jnp.sum(jnp.exp(logits - row_top[:, None]), axis=1), picked_her...  138 us
    psum x1, waiting for transfers between devices, per_device(): logits = lax.psum(logit_part, 'seq')  118 us
    pmax x1, blocking collectives, head_terms(): row_top = lax.pmax(jnp.max(logits, axis=1), ('grp', 'voc'))  75.6 us
    psum x1, blocking collectives, per_device(): squares = lax.psum(jnp.sum(own_rows * own_rows, axis=1), 'seq')  28.2 us
  transfers between devices with their start and end apart: 3, of which 3 were waited for; matrix products, arithmetic and copies ran while one was open for 1% of the time, Pallas kernels for 0%

commit v1 on v0

v1 whole, which is shorter than its diff:
```python
import functools

import jax
import jax.numpy as jnp
from jax import lax
from jax.experimental import pallas as pl
from jax.experimental.pallas import tpu as pltpu
from jax.sharding import PartitionSpec as P

EPSILON = 1e-05
GRAD_SCALE = 8.0
NX = 4
ROWS = 16
SKEW = 4
LANES = 128
F32 = jnp.float32
BF16 = jnp.bfloat16


def as_rows(columns):
    n = columns.shape[0]
    if n < LANES:
        columns = jnp.concatenate([columns, jnp.zeros((LANES - n, LANES), F32)], axis=0)
    return columns.T[:8]


def as_columns(rows, n):
    full = jnp.concatenate([rows, jnp.zeros((LANES - 8, LANES), F32)], axis=0)
    return full.T[:n]


def stack_rows(*rows):
    index = lax.broadcasted_iota(jnp.int32, (8, LANES), 0)
    out = jnp.zeros((8, LANES), F32)
    for i, row in enumerate(rows):
        out = jnp.where(index == i, jnp.broadcast_to(row, (8, LANES)), out)
    return out


def combine(tiles):
    top = tiles[0][0:1]
    for t in tiles[1:]:
        top = jnp.maximum(top, t[0:1])
    total = jnp.zeros_like(top)
    picked = jnp.zeros_like(top)
    for t in tiles:
        total = total + t[1:2] * jnp.exp(t[0:1] - top)
        picked = picked + t[2:3]
    return top, total, picked


def kernel(
    ny, nz, nc, res_ref, gain_ref, w_ref, tok_ref,
    loss_ref, head_ref, hid_ref,
    sqc, sqz, H, L, xs, xr, cs, cr, lg, dyb, dxb, DL, PB, g1, g2, gs, qf, qs, qr, acc, lossc, lossz,
    ssem, rsem,
):
    grp, seq, voc = lax.axis_index("grp"), lax.axis_index("seq"), lax.axis_index("voc")
    x, y = lax.div(voc, 2), grp * 2 + lax.rem(voc, 2)
    z, c = lax.div(seq, 2), lax.rem(seq, 2)
    oc = 1 - c
    vl, dl_width = w_ref.shape
    d_total = dl_width * nz * 2
    tp = ROWS * NX * ny // (nz * 2)
    half = ny // 2
    left, right, opp = lax.rem(x + 3, NX), lax.rem(x + 1, NX), lax.rem(x + 2, NX)

    def dev(x=x, y=y, z=z, c=c):
        return {"grp": lax.div(y, 2), "seq": z * 2 + c, "voc": x * 2 + lax.rem(y, 2)}

    ys = [lax.rem(y + d, ny) for d in range(1, ny)]
    zs = [lax.rem(z + d, nz) for d in range(1, nz)]
    xs_ = [lax.rem(x + d, NX) for d in range(1, NX)]

    started = []

    def send(src, dst, target):
        i = len(started)
        cp = pltpu.make_async_remote_copy(
            src_ref=src, dst_ref=dst, send_sem=ssem.at[i], recv_sem=rsem.at[i],
            device_id=target, device_id_type=pl.DeviceIdType.MESH,
        )
        cp.start()
        started.append(cp)
        return cp

    def arrive(copies):
        for cp in copies:
            cp.wait_recv()

    barrier = pltpu.get_barrier_semaphore()
    partners = (
        [dev(y=t) for t in ys] + [dev(z=t) for t in zs] + [dev(x=t) for t in xs_] + [dev(c=oc)]
    )
    for p in partners:
        pl.semaphore_signal(barrier, inc=1, device_id=p, device_id_type=pl.DeviceIdType.MESH)

    own = res_ref[...].astype(F32)
    n_own = own.shape[0]
    sq = own * own
    part = sq[:, :LANES]
    for j in range(LANES, dl_width, LANES):
        part = part + sq[:, j : j + LANES]
    part = jnp.concatenate([part, jnp.zeros((LANES - n_own, LANES), F32)], axis=0)
    sqc[c] = jnp.broadcast_to(jnp.sum(part.T, axis=0, keepdims=True), (8, LANES))
    pl.semaphore_wait(barrier, len(partners))
    arrive([send(sqc.at[c], sqc.at[c], dev(c=oc))])
    sqz[z] = sqc[0] + sqc[1]
    arrive([send(sqz.at[z], sqz.at[z], dev(z=t)) for t in zs])
    squares = sqz[0]
    for i in range(1, nz):
        squares = squares + sqz[i]
    inv = lax.rsqrt(squares / d_total + EPSILON)
    inv = jnp.broadcast_to(inv[0:1], (LANES, LANES)).T[:n_own]
    inv = jnp.concatenate([inv] * (dl_width // LANES), axis=1)
    hidden = (own * inv * gain_ref[...]).astype(BF16)
    gathers = []
    for k in range(nc):
        H[k, x, y] = hidden[k * ROWS : (k + 1) * ROWS]
        gathers.append([send(H.at[k, x, y], H.at[k, x, y], dev(y=t)) for t in ys])

    lane = lax.broadcasted_iota(jnp.int32, (1, LANES), 1)
    losses = []
    zt = half

    def chunk(k):
        arrive(gathers[k])
        a = [send(H.at[k, x], H.at[k, x], dev(x=t)) for t in (right, left)]
        yield
        arrive(a)
        a = [
            send(H.at[k, left, pl.ds(0, half)], H.at[k, left, pl.ds(0, half)], dev(x=right)),
            send(H.at[k, right, pl.ds(half, half)], H.at[k, right, pl.ds(half, half)], dev(x=left)),
        ]
        yield
        arrive(a)

        @pl.loop(0, NX // 2)
        def _(i):
            h = H[k, pl.ds(2 * i, 2)].reshape(2 * ny * ROWS, dl_width)
            t = lax.dot_general(h, w_ref[...], (((1,), (1,)), ((), ())), preferred_element_type=F32)
            L[k, pl.ds(zt * i, zt)] = t.reshape(zt, 2, tp, vl)

        for i in range(nz):
            xs[k, i] = L[k, i, oc].astype(BF16)
        a = [send(xs.at[k], xr.at[k], dev(c=oc))]
        yield
        arrive(a)
        for i in range(nz):
            cs[k, i] = (L[k, i, c] + xr[k, i].astype(F32)).astype(BF16)
        a = [send(cs.at[k, t], cr.at[k, z], dev(z=t)) for t in zs]
        yield
        arrive(a)
        logits = L[k, z, c] + xr[k, z].astype(F32)
        for t in zs:
            logits = logits + cr[k, t].astype(F32)
        lg[k] = logits

        tok = tok_ref[k]
        first_row = ((grp * NX * 2 + voc) * vl).astype(F32)
        column = lax.broadcasted_iota(jnp.int32, (tp, vl), 1).astype(F32)
        taken = column == as_columns(tok, tp)[:, 0:1] - first_row
        top = jnp.max(logits, axis=1, keepdims=True)
        total = jnp.sum(jnp.exp(logits - top), axis=1, keepdims=True)
        picked = jnp.sum(jnp.where(taken, logits, 0.0), axis=1, keepdims=True)
        at = lax.broadcasted_iota(jnp.int32, (tp, LANES), 1)
        dyb[k, y] = as_rows(
            jnp.where(at == 0, top, jnp.where(at == 1, total, jnp.where(at == 2, picked, 0.0)))
        )
        a = [send(dyb.at[k, y], dyb.at[k, y], dev(y=t)) for t in ys]
        yield
        arrive(a)
        dxb[k, x] = stack_rows(*combine([dyb[k, i] for i in range(ny)]))
        a = [send(dxb.at[k, x], dxb.at[k, x], dev(x=t)) for t in xs_]
        yield
        arrive(a)
        top, total, picked = combine([dxb[k, i] for i in range(NX)])
        is_own = lane < tp
        log_norm = top + jnp.log(jnp.where(is_own, total, 1.0))
        log_prob = picked - log_norm
        ratio = jnp.minimum(jnp.exp(log_prob - tok[1:2]), tok[4:5])
        scaled = tok[3:4] * ratio * tok[2:3]
        losses.append(jnp.sum(jnp.where(is_own, scaled * log_prob, 0.0), axis=1, keepdims=True))
        cols = as_columns(stack_rows(log_norm, GRAD_SCALE * scaled, tok[0:1]), tp)
        taken = column == cols[:, 2:3] - first_row
        softmax = jnp.exp(lg[k] - cols[:, 0:1])
        DL[k, z, c] = (cols[:, 1:2] * (softmax - taken.astype(F32))).astype(BF16)
        a = [send(DL.at[k, z, c], DL.at[k, z, c], dev(z=t)) for t in zs]
        last = k == nc - 1
        if last:
            lossc[c] = jnp.broadcast_to(sum(losses[1:], losses[0]), (8, LANES))
            b = [send(lossc.at[c], lossc.at[c], dev(c=oc))]
        yield
        arrive(a)
        a = [send(DL.at[k, :, c], DL.at[k, :, c], dev(c=oc))]
        if last:
            arrive(b)
            lossz[z] = lossc[0] + lossc[1]
            b = [send(lossz.at[z], lossz.at[z], dev(z=t)) for t in zs]
        yield
        arrive(a)

        @pl.loop(0, NX // 2)
        def _(i):
            d = DL[k, pl.ds(zt * i, zt)].reshape(2 * ny * ROWS, vl)
            t = jnp.dot(d, w_ref[...], preferred_element_type=F32).astype(BF16)
            PB[k, pl.ds(2 * i, 2)] = t.reshape(2, ny, ROWS, dl_width)

        low, high = pl.ds(0, half), pl.ds(half, half)
        a = [
            send(PB.at[k, opp, low], g1.at[k, 0], dev(x=left)),
            send(PB.at[k, opp, high], g1.at[k, 1], dev(x=right)),
        ]
        b2 = [
            send(PB.at[k, left, high], g2.at[k, 0, high], dev(x=left)),
            send(PB.at[k, right, low], g2.at[k, 1, low], dev(x=right)),
        ]
        h_all = H[k].reshape(NX * ny * ROWS, dl_width)
        d_all = DL[k].reshape(NX * ny * ROWS, vl)
        t = lax.dot_general(d_all, h_all, (((0,), (0,)), ((), ())), preferred_element_type=F32)
        if nc == 1:
            head_ref[...] = t.astype(BF16)
        elif k == 0:
            acc[...] = t
        elif last:
            head_ref[...] = (acc[...] + t).astype(BF16)
        else:
            acc[...] += t
        yield
        arrive(a)
        gs[k, 0] = (PB[k, left, low].astype(F32) + g1[k, 0].astype(F32)).astype(BF16)
        b2.append(send(gs.at[k, 0], g2.at[k, 0, low], dev(x=left)))
        gs[k, 1] = (PB[k, right, high].astype(F32) + g1[k, 1].astype(F32)).astype(BF16)
        b2.append(send(gs.at[k, 1], g2.at[k, 1, high], dev(x=right)))
        yield
        arrive(b2)
        for i in range(ny):
            q = PB[k, x, i].astype(F32) + g2[k, 0, i].astype(F32) + g2[k, 1, i].astype(F32)
            qf[k, i] = q
            qs[k, i] = q.astype(BF16)
        a = [send(qs.at[k, t], qr.at[k, y], dev(y=t)) for t in ys]
        yield
        arrive(a)
        q = qf[k, y]
        for t in ys:
            q = q + qr[k, t].astype(F32)
        hid_ref[k * ROWS : (k + 1) * ROWS, :] = q
        if last:
            arrive(b)
            loss = lossz[0]
            for i in range(1, nz):
                loss = loss + lossz[i]
            loss_ref[...] = loss * (-1.0 / (n_own * NX * ny))

    runs = [chunk(k) for k in range(nc)]
    slot = 0
    while any(r is not None for r in runs):
        for k in range(nc):
            if slot >= k * SKEW and runs[k] is not None:
                try:
                    next(runs[k])
                except StopIteration:
                    runs[k] = None
        slot += 1
    for cp in started:
        cp.wait_send()


def per_device(mesh_sizes, residual, norm_gain, head_weight, actions, behavior_logp, advantages, decision_mask, clip_tenths):
    n_grp, n_seq, n_voc = mesh_sizes
    ny, nz = n_grp * 2, n_seq // 2
    n_own, dw = residual.shape
    vl = head_weight.shape[0]
    nc = n_own // ROWS
    tp = ROWS * NX * ny // n_seq

    seq = lax.axis_index("seq")
    pairs = [actions.astype(F32), behavior_logp, advantages, decision_mask.astype(F32), clip_tenths.astype(F32) / 10.0]
    tok = jnp.stack(pairs).reshape(5, n_seq, 2, nc, ROWS)
    where = lax.rem(2 * seq, ny) // 2 * NX + lax.div(2 * seq, ny)
    tok = lax.dynamic_index_in_dim(tok, where, 1, keepdims=False)
    tok = tok.transpose(2, 0, 1, 3).reshape(nc, 5, tp)
    tok = jnp.pad(tok, ((0, 0), (0, 3), (0, LANES - tp)))

    n_sends = (1 + nz - 1) + nc * (3 * (ny - 1) + 2 * (nz - 1) + 2 + 2 + 1 + 3 + 1 + 6) + 1 + nz - 1
    vm = pl.BlockSpec(memory_space=pltpu.VMEM)
    tile = (8, LANES)
    loss, head_grad, hidden_grad = pl.pallas_call(
        functools.partial(kernel, ny, nz, nc),
        out_shape=(
            jax.ShapeDtypeStruct(tile, F32),
            jax.ShapeDtypeStruct((vl, dw), BF16),
            jax.ShapeDtypeStruct((n_own, dw), F32),
        ),
        in_specs=[vm] * 4,
        out_specs=(vm, vm, vm),
        scratch_shapes=[
            pltpu.VMEM((2,) + tile, F32),
            pltpu.VMEM((nz,) + tile, F32),
            pltpu.VMEM((nc, NX, ny, ROWS, dw), BF16),
            pltpu.VMEM((nc, nz, 2, tp, vl), F32),
            pltpu.VMEM((nc, nz, tp, vl), BF16),
            pltpu.VMEM((nc, nz, tp, vl), BF16),
            pltpu.VMEM((nc, nz, tp, vl), BF16),
            pltpu.VMEM((nc, nz, tp, vl), BF16),
            pltpu.VMEM((nc, tp, vl), F32),
            pltpu.VMEM((nc, ny) + tile, F32),
            pltpu.VMEM((nc, NX) + tile, F32),
            pltpu.VMEM((nc, nz, 2, tp, vl), BF16),
            pltpu.VMEM((nc, NX, ny, ROWS, dw), BF16),
            pltpu.VMEM((nc, 2, ny // 2, ROWS, dw), BF16),
            pltpu.VMEM((nc, 2, ny, ROWS, dw), BF16),
            pltpu.VMEM((nc, 2, ny // 2, ROWS, dw), BF16),
            pltpu.VMEM((nc, ny, ROWS, dw), F32),
            pltpu.VMEM((nc, ny, ROWS, dw), BF16),
            pltpu.VMEM((nc, ny, ROWS, dw), BF16),
            pltpu.VMEM((vl, dw), F32),
            pltpu.VMEM((2,) + tile, F32),
            pltpu.VMEM((nz,) + tile, F32),
            pltpu.SemaphoreType.DMA((n_sends,)),
            pltpu.SemaphoreType.DMA((n_sends,)),
        ],
        compiler_params=pltpu.CompilerParams(
            collective_id=0, has_side_effects=True, vmem_limit_bytes=56 * 2**20
        ),
    )(residual, norm_gain.reshape(1, dw), head_weight, tok)
    return loss[0, 0], head_grad, hidden_grad


def solution(mesh):
    sizes = (mesh.shape["grp"], mesh.shape["seq"], mesh.shape["voc"])
    split = P(("grp", "voc"), "seq")
    return jax.shard_map(
        functools.partial(per_device, sizes),
        mesh=mesh,
        in_specs=(split, P("seq"), split, P(), P(), P(), P(), P()),
        out_specs=(P(), split, split),
        check_vma=False,
    )
```

time: 696 us -> 147 us (0.21)
  the two profiles are of different devices: /device:TPU:64 before, /device:TPU:1 now
where the time goes in v1:
time: 147 us; the launch traced here: 146 us
  Pallas kernels  136 us (93%)
  local copies, waits for them, and re-layouts  9.07 us (6%)
    pallas_call x1, Pallas kernels, per_device(): pl.pallas_call(functools.partial(kernel, ny, nz, nc), out_shape=(jax.Shap...  136 us
    unnamed x20, local copies, waits for them, and re-layouts  6.07 us

profile of v1, /device:TPU:1, one launch (start us, length us, event | category | flops | bytes accessed | tf_op | source)
XLA Modules:
  0.0 146.3 jit_solution(1318027560375380514)
XLA Ops:
  0.7 0.0 copy-start.6
  0.7 0.0 copy-start.3
  0.7 0.7 copy-done.6
  1.3 0.6 reshape.23.gain_ref
  1.9 0.0 copy-done.3
  1.9 0.0 copy-start.4
  1.9 0.7 copy-done.4
  2.6 0.0 copy-start.5
  2.6 0.7 copy-done.5
  3.3 0.1 stack.22
  3.4 0.1 stack.21
  3.5 0.0 copy-start.1
  3.5 0.1 stack.18
  3.6 0.6 copy-done.1
  4.2 0.1 stack.19
  4.3 0.6 copy-done.2
  4.9 0.1 stack.20
  5.2 0.1 reshape.24
  5.3 0.6 pad.4.tok_ref
  5.9 136.4 %shard_map.103 = (f32[8,128]{1,0:T(8,128)}, bf16[512,768]{1,0:T(8,128)(2,1)}, f32[48,768]{1,0:T(8,128)}) custom-call(bf16[48,768]{1,0:T(8,128)(2,1)} %res_ref.1, f32[1,768]{1,0:T(1,128)} %reshape.23.gain_ref, bf16[512,768]{1,0:T(8,128)(2,1)} %w_ref.1, f32[3,8,128]{2,1,0:T(8,128)} %pad.4.tok_ref), custom_call_target="tpu_custom_call" | custom-call | tf_op jit(solution)/shard_map/pallas_call | solution.py:288
  142.3 1.2 slice.3
  143.5 2.1 %copy.22 = bf16[512,768]{1,0:T(8,128)(2,1)} copy(bf16[512,768]{1,0:T(8,128)(2,1)} %get-tuple-element.13) | data formatting | bytes 1572864
  145.6 0.0 copy-done
  145.6 0.7 copy.23
  (13 shorter events, 0.1 us)
Async XLA Ops:
  0.7 0.7 copy-start.6
  0.7 1.3 copy-start.3
  1.9 0.7 copy-start.4
  2.6 0.7 copy-start.5
  3.5 0.7 copy-start.1
  4.2 0.7 copy-start.2
  143.5 2.1 %copy-start = (f32[48,768]{1,0:T(8,128)S(1)}, f32[48,768]{1,0:T(8,128)}, u32[]{:S(2)}) copy-start(f32[48,768]{1,0:T(8,128)} %get-tuple-element.14) | copy-start | bytes 442372

commit v2 on v1

v2 whole, which is shorter than its diff:
```python
import functools

import jax
import jax.numpy as jnp
from jax import lax
from jax.experimental import pallas as pl
from jax.experimental.pallas import tpu as pltpu
from jax.sharding import PartitionSpec as P

EPSILON = 1e-05
GRAD_SCALE = 8.0
NX = 4
ROWS = 16
STAGGER = 6.0
READY = (7.0, 13.5, 16.2, 17.0, 18.5, 19.5, 24.0, 25.0, 31.0, 34.5, 43.0, 44.5, 50.0, 56.5, 64.0)
NORM_READY = (0.9, 6.5, 12.2, 16.0)
FAR_FIRST = (4, 3, 5, 2, 6, 1, 7)
LANES = 128
F32 = jnp.float32
BF16 = jnp.bfloat16


def as_rows(columns):
    n = columns.shape[0]
    if n < LANES:
        columns = jnp.concatenate([columns, jnp.zeros((LANES - n, LANES), F32)], axis=0)
    return columns.T[:8]


def as_columns(rows, n):
    full = jnp.concatenate([rows, jnp.zeros((LANES - 8, LANES), F32)], axis=0)
    return full.T[:n]


def stack_rows(*rows):
    index = lax.broadcasted_iota(jnp.int32, (8, LANES), 0)
    out = jnp.zeros((8, LANES), F32)
    for i, row in enumerate(rows):
        out = jnp.where(index == i, jnp.broadcast_to(row, (8, LANES)), out)
    return out


def combine(tiles):
    top = tiles[0][0:1]
    for t in tiles[1:]:
        top = jnp.maximum(top, t[0:1])
    total = jnp.zeros_like(top)
    picked = jnp.zeros_like(top)
    for t in tiles:
        total = total + t[1:2] * jnp.exp(t[0:1] - top)
        picked = picked + t[2:3]
    return top, total, picked


def kernel(
    ny, nz, nc,
    res_hbm, gain_hbm, w_hbm, act_hbm, beh_hbm, adv_hbm, mask_hbm, clip_hbm,
    loss_ref, head_ref, hid_ref,
    res, gain, w, act, beh, adv, mask, clip, tk,
    sqc, sqz, iny, inx, invc, H, HH, Lo, xs, xr, cs, cr, lg, dcb, dyb, dxb, DL, PB,
    g1, g2, gs, qf, qs, qr, lossz, lsem, ssem, rsem,
):
    grp, seq, voc = lax.axis_index("grp"), lax.axis_index("seq"), lax.axis_index("voc")
    x, y = lax.div(voc, 2), grp * 2 + lax.rem(voc, 2)
    z, c = lax.div(seq, 2), lax.rem(seq, 2)
    oc = 1 - c
    vl, dw = w.shape
    vh = vl // 2
    tp = ROWS * NX
    n_own = res.shape[0]
    half = ny // 2
    left, right, opp = lax.rem(x + 3, NX), lax.rem(x + 1, NX), lax.rem(x + 2, NX)
    order = (x, left, right, opp)

    def dev(x=x, y=y, z=z, c=c):
        return {"grp": lax.div(y, 2), "seq": z * 2 + c, "voc": x * 2 + lax.rem(y, 2)}

    ys = [lax.rem(y + d, ny) for d in FAR_FIRST if d < ny]
    zs = [lax.rem(z + d, nz) for d in FAR_FIRST if d < nz]
    others = [opp, right, left]

    loads = []
    pairs = ((res_hbm, res), (gain_hbm, gain), (w_hbm, w), (act_hbm, act), (beh_hbm, beh),
             (adv_hbm, adv), (mask_hbm, mask), (clip_hbm, clip))
    for i, (src, dst) in enumerate(pairs):
        loads.append(pltpu.make_async_copy(src, dst, lsem.at[i]))
        loads[-1].start()

    started = []

    def send(src, dst, target):
        i = len(started)
        cp = pltpu.make_async_remote_copy(
            src_ref=src, dst_ref=dst, send_sem=ssem.at[i], recv_sem=rsem.at[i],
            device_id=target, device_id_type=pl.DeviceIdType.MESH,
        )
        cp.start()
        started.append(cp)
        return cp

    def arrive(copies):
        for cp in copies:
            cp.wait_recv()

    barrier = pltpu.get_barrier_semaphore()
    partners = (
        [dev(y=t) for t in ys] + [dev(z=t) for t in zs] + [dev(x=t) for t in others] + [dev(c=oc)]
    )
    for p in partners:
        pl.semaphore_signal(barrier, inc=1, device_id=p, device_id_type=pl.DeviceIdType.MESH)

    loads[0].wait()
    sq = res[...].astype(F32)
    sq = sq * sq
    part = sq[:, :LANES]
    for j in range(LANES, dw, LANES):
        part = part + sq[:, j : j + LANES]
    part = jnp.concatenate([part, jnp.zeros((LANES - n_own, LANES), F32)], axis=0)
    sqc[c] = jnp.broadcast_to(jnp.sum(part.T, axis=0, keepdims=True), (8, LANES))
    for k in range(nc):
        H[k, x, y] = res[k * ROWS : (k + 1) * ROWS]
    pl.semaphore_wait(barrier, len(partners))

    gathers = {}

    def gather_y(k):
        gathers[k] = [send(H.at[k, x, y], H.at[k, x, y], dev(y=t)) for t in ys]

    def norm():
        a = [send(sqc.at[c], sqc.at[c], dev(c=oc))]
        gather_y(0)
        for cp in loads[1:]:
            cp.wait()
        n = tk.shape[0]
        vectors = [v[...].astype(F32).reshape(n, LANES) for v in (act, beh, adv, mask, clip)]
        vectors[4] = vectors[4] / 10.0
        for i in range(n):
            tk[i] = stack_rows(*[v[i : i + 1] for v in vectors])
        yield
        arrive(a)
        sqz[z] = sqc[0] + sqc[1]
        a = [send(sqz.at[z], sqz.at[z], dev(z=t)) for t in zs]
        yield
        arrive(a)
        squares = sqz[0]
        for i in range(1, nz):
            squares = squares + sqz[i]
        iny[y] = lax.rsqrt(squares / (dw * nz * 2) + EPSILON)
        a = [send(iny.at[y], iny.at[y], dev(y=t)) for t in ys]
        yield
        arrive(a)
        inx[x] = stack_rows(*[iny[i, 0:1] for i in range(ny)])
        a = [send(inx.at[x], inx.at[x], dev(x=t)) for t in others]
        yield
        arrive(a)
        rows = jnp.concatenate(
            [inx[i] for i in range(NX)] + [jnp.zeros((LANES - 8 * NX, LANES), F32)], axis=0
        )
        columns = rows.T
        for i in range(NX):
            invc[i] = pltpu.roll(columns, (LANES - 8 * i) % LANES, 1) if i else columns

    lane = lax.broadcasted_iota(jnp.int32, (8, LANES), 1)
    losses = []
    first_row = ((grp * NX * 2 + voc) * vl + c * vh).astype(F32)

    def own_tokens(k):
        out = jnp.zeros((8, LANES), F32)
        for i in range(NX):
            block = lax.div(z, 2) * (NX * 2) + i * 2 + lax.rem(z, 2)
            at = block * n_own + k * ROWS
            shift = lax.rem(LANES + i * ROWS - lax.rem(at, LANES), LANES)
            t = pltpu.roll(tk[lax.div(at, LANES)], shift, 1)
            out = jnp.where((lane >= i * ROWS) & (lane < (i + 1) * ROWS), t, out)
        return out

    def terms(k, pos):
        at = order[pos]
        cols = invc[at]
        for j in range(ny):
            unit = H[k, at, j].astype(F32) * cols[k * ROWS : (k + 1) * ROWS, j : j + 1]
            HH[k, at, j] = (unit * gain[...].reshape(1, dw)).astype(BF16)
        h = HH[k, at].reshape(ny * ROWS, dw)
        w_other = w[pl.ds(pl.multiple_of(oc * vh, vh), vh)]
        t = lax.dot_general(h, w_other, (((1,), (1,)), ((), ())), preferred_element_type=F32)
        xs[k, pos] = t.astype(BF16).reshape(ny, ROWS, vh)
        cp = send(xs.at[k, pos], xr.at[k, pos], dev(c=oc))
        w_own = w[pl.ds(pl.multiple_of(c * vh, vh), vh)]
        t = lax.dot_general(h, w_own, (((1,), (1,)), ((), ())), preferred_element_type=F32)
        Lo[k, pos] = t.reshape(ny, ROWS, vh)
        return cp

    def chunk(k):
        last = k == nc - 1
        arrive(gathers[k])
        a = [send(H.at[k, x], H.at[k, x], dev(x=t)) for t in (right, left)]
        if not last:
            gather_y(k + 1)
        yield
        arrive(a)
        low, high = pl.ds(0, half), pl.ds(half, half)
        a = [
            send(H.at[k, left, low], H.at[k, left, low], dev(x=right)),
            send(H.at[k, right, high], H.at[k, right, high], dev(x=left)),
        ]
        yield
        b = [terms(k, pos) for pos in range(NX - 1)]
        yield
        arrive(b)
        near = pl.ds(0, NX - 1)
        b = []
        for t in zs + [z]:
            for pos in range(NX - 1):
                cs[k, t, pos] = (Lo[k, pos, t] + xr[k, pos, t].astype(F32)).astype(BF16)
        for t in zs:
            b.append(send(cs.at[k, t, near], cr.at[k, z, near], dev(z=t)))
        yield
        arrive(a)
        a = [terms(k, NX - 1)]
        yield
        arrive(a)
        far = NX - 1
        for t in zs:
            cs[k, t, far] = (Lo[k, far, t] + xr[k, far, t].astype(F32)).astype(BF16)
            b.append(send(cs.at[k, t, far], cr.at[k, z, far], dev(z=t)))
        yield
        arrive(b)
        for pos in range(NX):
            logits = Lo[k, pos, z] + xr[k, pos, z].astype(F32)
            for t in zs:
                logits = logits + cr[k, t, pos].astype(F32)
            lg[k, order[pos]] = logits
        logits = lg[k].reshape(tp, vh)

        tok = own_tokens(k)
        column = lax.broadcasted_iota(jnp.int32, (tp, vh), 1).astype(F32)
        taken = column == as_columns(tok, tp)[:, 0:1] - first_row
        top = jnp.max(logits, axis=1, keepdims=True)
        total = jnp.sum(jnp.exp(logits - top), axis=1, keepdims=True)
        picked = jnp.sum(jnp.where(taken, logits, 0.0), axis=1, keepdims=True)
        at = lax.broadcasted_iota(jnp.int32, (tp, LANES), 1)
        dcb[k, c] = as_rows(
            jnp.where(at == 0, top, jnp.where(at == 1, total, jnp.where(at == 2, picked, 0.0)))
        )
        a = [send(dcb.at[k, c], dcb.at[k, c], dev(c=oc))]
        yield
        arrive(a)
        dyb[k, y] = stack_rows(*combine([dcb[k, 0], dcb[k, 1]]))
        a = [send(dyb.at[k, y], dyb.at[k, y], dev(y=t)) for t in ys]
        yield
        arrive(a)
        dxb[k, x] = stack_rows(*combine([dyb[k, i] for i in range(ny)]))
        a = [send(dxb.at[k, x], dxb.at[k, x], dev(x=t)) for t in others]
        yield
        arrive(a)
        top, total, picked = combine([dxb[k, i] for i in range(NX)])
        is_own = lane[0:1] < tp
        log_norm = top + jnp.log(jnp.where(is_own, total, 1.0))
        log_prob = picked - log_norm
        ratio = jnp.minimum(jnp.exp(log_prob - tok[1:2]), tok[4:5])
        scaled = tok[3:4] * ratio * tok[2:3]
        losses.append(jnp.sum(jnp.where(is_own, scaled * log_prob, 0.0), axis=1, keepdims=True))
        cols = as_columns(stack_rows(log_norm, GRAD_SCALE * scaled, tok[0:1]), tp)
        taken = column == cols[:, 2:3] - first_row
        softmax = jnp.exp(lg[k].reshape(tp, vh) - cols[:, 0:1])
        dl = (cols[:, 1:2] * (softmax - taken.astype(F32))).astype(BF16)
        for i in range(NX):
            DL[k, c, i, z] = dl[i * ROWS : (i + 1) * ROWS]
        a = [send(DL.at[k, c, :, z], DL.at[k, c, :, z], dev(z=t)) for t in zs]
        if last:
            lossz[z] = jnp.broadcast_to(sum(losses[1:], losses[0]), (8, LANES))
            b = [send(lossz.at[z], lossz.at[z], dev(z=t)) for t in zs]
        yield
        arrive(a)
        a = [send(DL.at[k, c], DL.at[k, c], dev(c=oc))]
        yield
        arrive(a)

        def term(at):
            d0 = DL[k, 0, at].reshape(ny * ROWS, vh)
            d1 = DL[k, 1, at].reshape(ny * ROWS, vh)
            t = jnp.dot(d0, w[0:vh], preferred_element_type=F32)
            t = t + jnp.dot(d1, w[vh:vl], preferred_element_type=F32)
            PB[k, at] = t.astype(BF16).reshape(ny, ROWS, dw)

        term(opp)
        a = [
            send(PB.at[k, opp, low], g1.at[k, 0], dev(x=left)),
            send(PB.at[k, opp, high], g1.at[k, 1], dev(x=right)),
        ]
        term(left)
        b2 = [send(PB.at[k, left, high], g2.at[k, 0, high], dev(x=left))]
        term(right)
        b2.append(send(PB.at[k, right, low], g2.at[k, 1, low], dev(x=right)))
        term(x)
        yield
        arrive(a)
        gs[k, 0] = (PB[k, left, low].astype(F32) + g1[k, 0].astype(F32)).astype(BF16)
        b2.append(send(gs.at[k, 0], g2.at[k, 0, low], dev(x=left)))
        gs[k, 1] = (PB[k, right, high].astype(F32) + g1[k, 1].astype(F32)).astype(BF16)
        b2.append(send(gs.at[k, 1], g2.at[k, 1, high], dev(x=right)))
        if last:
            h_all = HH[...].reshape(nc * NX * ny * ROWS, dw)
            for i in range(2):
                d_all = DL[:, i].reshape(nc * NX * ny * ROWS, vh)
                t = lax.dot_general(
                    d_all, h_all, (((0,), (0,)), ((), ())), preferred_element_type=F32
                )
                head_ref[i * vh : (i + 1) * vh, :] = t.astype(BF16)
        yield
        arrive(b2)
        for t in ys + [y]:
            q = PB[k, x, t].astype(F32) + g2[k, 0, t].astype(F32) + g2[k, 1, t].astype(F32)
            qf[k, t] = q
            qs[k, t] = q.astype(BF16)
        a = [send(qs.at[k, t], qr.at[k, y], dev(y=t)) for t in ys]
        yield
        arrive(a)
        q = qf[k, y]
        for t in ys:
            q = q + qr[k, t].astype(F32)
        hid_ref[k * ROWS : (k + 1) * ROWS, :] = q
        if last:
            arrive(b)
            loss = lossz[0]
            for i in range(1, nz):
                loss = loss + lossz[i]
            loss_ref[0, 0] = jnp.max(loss[0:1]) * (-1.0 / (n_own * NX * ny))

    plan = [(t, -1) for t in (0.0,) + NORM_READY]
    plan += [(t + STAGGER * k, k) for k in range(nc) for t in READY]
    runs = {-1: norm()}
    runs.update((k, chunk(k)) for k in range(nc))
    for _, k in sorted(plan):
        next(runs[k], None)
    for cp in started:
        cp.wait_send()


def per_device(mesh_sizes, residual, norm_gain, head_weight, actions, behavior_logp, advantages, decision_mask, clip_tenths):
    n_grp, n_seq, n_voc = mesh_sizes
    ny, nz = n_grp * 2, n_seq // 2
    n_own, dw = residual.shape
    vl = head_weight.shape[0]
    tokens = actions.shape[0]
    nc = n_own // ROWS
    vh = vl // 2

    per_chunk = 4 * (ny - 1) + 3 * (nz - 1) + 2 + 2 + NX + 1 + (NX - 1) + 1 + 6
    n_sends = 1 + (nz - 1) + (ny - 1) + (NX - 1) + nc * per_chunk + nz - 1
    any_space = pl.BlockSpec(memory_space=pl.ANY)
    vm = pl.BlockSpec(memory_space=pltpu.VMEM)
    tile = (8, LANES)
    loss, head_grad, hidden_grad = pl.pallas_call(
        functools.partial(kernel, ny, nz, nc),
        out_shape=(
            jax.ShapeDtypeStruct((1, 1), F32),
            jax.ShapeDtypeStruct((vl, dw), BF16),
            jax.ShapeDtypeStruct((n_own, dw), F32),
        ),
        in_specs=[any_space] * 8,
        out_specs=(pl.BlockSpec(memory_space=pltpu.SMEM), vm, vm),
        scratch_shapes=[
            pltpu.VMEM((n_own, dw), BF16),
            pltpu.VMEM((dw,), F32),
            pltpu.VMEM((vl, dw), BF16),
            pltpu.VMEM((tokens,), jnp.int32),
            pltpu.VMEM((tokens,), F32),
            pltpu.VMEM((tokens,), F32),
            pltpu.VMEM((tokens,), jnp.int32),
            pltpu.VMEM((tokens,), jnp.int32),
            pltpu.VMEM((tokens // LANES,) + tile, F32),
            pltpu.VMEM((2,) + tile, F32),
            pltpu.VMEM((nz,) + tile, F32),
            pltpu.VMEM((ny,) + tile, F32),
            pltpu.VMEM((NX,) + tile, F32),
            pltpu.VMEM((NX, LANES, LANES), F32),
            pltpu.VMEM((nc, NX, ny, ROWS, dw), BF16),
            pltpu.VMEM((nc, NX, ny, ROWS, dw), BF16),
            pltpu.VMEM((nc, NX, ny, ROWS, vh), F32),
            pltpu.VMEM((nc, NX, ny, ROWS, vh), BF16),
            pltpu.VMEM((nc, NX, ny, ROWS, vh), BF16),
            pltpu.VMEM((nc, nz, NX, ROWS, vh), BF16),
            pltpu.VMEM((nc, nz, NX, ROWS, vh), BF16),
            pltpu.VMEM((nc, NX, ROWS, vh), F32),
            pltpu.VMEM((nc, 2) + tile, F32),
            pltpu.VMEM((nc, ny) + tile, F32),
            pltpu.VMEM((nc, NX) + tile, F32),
            pltpu.VMEM((nc, 2, NX, ny, ROWS, vh), BF16),
            pltpu.VMEM((nc, NX, ny, ROWS, dw), BF16),
            pltpu.VMEM((nc, 2, ny // 2, ROWS, dw), BF16),
            pltpu.VMEM((nc, 2, ny, ROWS, dw), BF16),
            pltpu.VMEM((nc, 2, ny // 2, ROWS, dw), BF16),
            pltpu.VMEM((nc, ny, ROWS, dw), F32),
            pltpu.VMEM((nc, ny, ROWS, dw), BF16),
            pltpu.VMEM((nc, ny, ROWS, dw), BF16),
            pltpu.VMEM((nz,) + tile, F32),
            pltpu.SemaphoreType.DMA((8,)),
            pltpu.SemaphoreType.DMA((n_sends,)),
            pltpu.SemaphoreType.DMA((n_sends,)),
        ],
        compiler_params=pltpu.CompilerParams(
            collective_id=0, has_side_effects=True, vmem_limit_bytes=60 * 2**20
        ),
    )(residual, norm_gain, head_weight, actions, behavior_logp, advantages, decision_mask, clip_tenths)
    return loss.reshape(()), head_grad, hidden_grad


def solution(mesh):
    sizes = (mesh.shape["grp"], mesh.shape["seq"], mesh.shape["voc"])
    split = P(("grp", "voc"), "seq")
    return jax.shard_map(
        functools.partial(per_device, sizes),
        mesh=mesh,
        in_specs=(split, P("seq"), split, P(), P(), P(), P(), P()),
        out_specs=(P(), split, split),
        check_vma=False,
    )
```

time: 147 us -> 107 us (0.73)
  Pallas kernels: 136 us -> 102 us
  local copies, waits for them, and re-layouts: 9.07 us -> 2.76 us
  between operations: 0.79 us -> 2.42 us
    pallas_call x1, Pallas kernels: 136 us -> 102 us  [per_device(): pl.pallas_call(functools.partial(kernel, ny, nz, nc), out_shape=(jax.Shap...]
    unnamed x20 -> x4, local copies, waits for them, and re-layouts: 6.07 us -> 2.76 us
where the time goes in v2:
time: 107 us
  Pallas kernels  102 us (95%)
  local copies, waits for them, and re-layouts  2.76 us (3%)
  between operations  2.42 us (2%)
    pallas_call x1, Pallas kernels, per_device(): pl.pallas_call(functools.partial(kernel, ny, nz, nc), out_shape=(jax.Shap...  102 us
    unnamed x4, local copies, waits for them, and re-layouts  2.76 us

profile of v2, /device:TPU:1, one launch (start us, length us, event | category | flops | bytes accessed | tf_op | source)
XLA Modules:
  0.0 107.0 jit_solution(14874168244917125283)
XLA Ops:
  0.6 101.8 %shard_map.103 = (f32[1,1]{1,0:T(1,128)}, bf16[512,768]{1,0:T(8,128)(2,1)}, f32[48,768]{1,0:T(8,128)}) custom-call(bf16[48,768]{1,0:T(8,128)(2,1)} %res_hbm.1, f32[768]{0:T(1024)} %gain_hbm.1, bf16[512,768]{1,0:T(8,128)(2,1)} %w_hbm.1, s32[1536]{0:T(1024)} %act_hbm.1, f32[1536]{0:T(1024)} %beh_hbm.1, f32[1536]{0:T(1024)} %adv_hbm.1, s32[1536]{0:T(1024)} %mask_hbm.1, ...), custom_call_target="tpu_custom_call" | custom-call | tf_op jit(solution)/shard_map/pallas_call | solution.py:354
  103.1 0.0 copy-start
  103.1 2.1 %copy.15 = bf16[512,768]{1,0:T(8,128)(2,1)} copy(bf16[512,768]{1,0:T(8,128)(2,1)} %get-tuple-element.13) | data formatting | bytes 1572864
  105.2 0.0 copy-done
  105.2 0.7 copy.16
Async XLA Ops:
  103.1 2.1 %copy-start = (f32[48,768]{1,0:T(8,128)S(1)}, f32[48,768]{1,0:T(8,128)}, u32[]{:S(2)}) copy-start(f32[48,768]{1,0:T(8,128)} %get-tuple-element.14) | copy-start | bytes 442372

commit v3 on v2

--- a/solution.py
+++ b/solution.py
@@ -11,9 +11,12 @@
 GRAD_SCALE = 8.0
 NX = 4
 ROWS = 16
-STAGGER = 6.0
-READY = (7.0, 13.5, 16.2, 17.0, 18.5, 19.5, 24.0, 25.0, 31.0, 34.5, 43.0, 44.5, 50.0, 56.5, 64.0)
-NORM_READY = (0.9, 6.5, 12.2, 16.0)
+NORM, GATHER, HEAD = -1, 3, 4
+PLAN = (
+    -1, -1, 0, -1, 3, 3, -1, 0, 1, -1, 0, 2, 0, 0, 1, 1, 0, 1, 2, 2, 1, 0, 1, 0,
+    2, 2, 2, 1, 0, 1, 0, 2, 1, 2, 0, 0, 1, 0, 2, 0, 0, 1, 2, 1, 1, 1, 2, 0,
+    2, 1, 2, 2, 2, 0, 1, 2, 4, 1, 2,
+)
 FAR_FIRST = (4, 3, 5, 2, 6, 1, 7)
 LANES = 128
 F32 = jnp.float32
@@ -57,7 +60,7 @@
     res_hbm, gain_hbm, w_hbm, act_hbm, beh_hbm, adv_hbm, mask_hbm, clip_hbm,
     loss_ref, head_ref, hid_ref,
     res, gain, w, act, beh, adv, mask, clip, tk,
-    sqc, sqz, iny, inx, invc, H, HH, Lo, xs, xr, cs, cr, lg, dcb, dyb, dxb, DL, PB,
+    sqc, sqz, iny, inx, invc, H, HH, Lo, xs, xr, cs, cr, lg, dcb, dyb, dxb, dlx, DL, PB,
     g1, g2, gs, qf, qs, qr, lossz, lsem, ssem, rsem,
 ):
     grp, seq, voc = lax.axis_index("grp"), lax.axis_index("seq"), lax.axis_index("voc")
@@ -179,8 +182,8 @@
         cols = invc[at]
         for j in range(ny):
             unit = H[k, at, j].astype(F32) * cols[k * ROWS : (k + 1) * ROWS, j : j + 1]
-            HH[k, at, j] = (unit * gain[...].reshape(1, dw)).astype(BF16)
-        h = HH[k, at].reshape(ny * ROWS, dw)
+            HH[k, pos, j] = (unit * gain[...].reshape(1, dw)).astype(BF16)
+        h = HH[k, pos].reshape(ny * ROWS, dw)
         w_other = w[pl.ds(pl.multiple_of(oc * vh, vh), vh)]
         t = lax.dot_general(h, w_other, (((1,), (1,)), ((), ())), preferred_element_type=F32)
         xs[k, pos] = t.astype(BF16).reshape(ny, ROWS, vh)
@@ -194,8 +197,6 @@
         last = k == nc - 1
         arrive(gathers[k])
         a = [send(H.at[k, x], H.at[k, x], dev(x=t)) for t in (right, left)]
-        if not last:
-            gather_y(k + 1)
         yield
         arrive(a)
         low, high = pl.ds(0, half), pl.ds(half, half)
@@ -265,52 +266,53 @@
         softmax = jnp.exp(lg[k].reshape(tp, vh) - cols[:, 0:1])
         dl = (cols[:, 1:2] * (softmax - taken.astype(F32))).astype(BF16)
         for i in range(NX):
-            DL[k, c, i, z] = dl[i * ROWS : (i + 1) * ROWS]
-        a = [send(DL.at[k, c, :, z], DL.at[k, c, :, z], dev(z=t)) for t in zs]
+            dlx[k, i] = dl[i * ROWS : (i + 1) * ROWS]
+        for pos in range(NX):
+            DL[k, c, pos, z] = dlx[k, order[pos]]
+        far, near = NX - 1, pl.ds(0, NX - 1)
+        a = [send(DL.at[k, c, far, z], DL.at[k, c, far, z], dev(z=t)) for t in zs]
+        d = [send(DL.at[k, c, near, z], DL.at[k, c, near, z], dev(z=t)) for t in zs]
         if last:
             lossz[z] = jnp.broadcast_to(sum(losses[1:], losses[0]), (8, LANES))
             b = [send(lossz.at[z], lossz.at[z], dev(z=t)) for t in zs]
         yield
         arrive(a)
-        a = [send(DL.at[k, c], DL.at[k, c], dev(c=oc))]
-        yield
-        arrive(a)
-
-        def term(at):
-            d0 = DL[k, 0, at].reshape(ny * ROWS, vh)
-            d1 = DL[k, 1, at].reshape(ny * ROWS, vh)
+        a = [send(DL.at[k, c, far], DL.at[k, c, far], dev(c=oc))]
+        yield
+        arrive(a)
+
+        def term(pos):
+            d0 = DL[k, 0, pos].reshape(ny * ROWS, vh)
+            d1 = DL[k, 1, pos].reshape(ny * ROWS, vh)
             t = jnp.dot(d0, w[0:vh], preferred_element_type=F32)
             t = t + jnp.dot(d1, w[vh:vl], preferred_element_type=F32)
-            PB[k, at] = t.astype(BF16).reshape(ny, ROWS, dw)
-
-        term(opp)
+            PB[k, pos] = t.astype(BF16).reshape(ny, ROWS, dw)
+
+        term(3)
         a = [
-            send(PB.at[k, opp, low], g1.at[k, 0], dev(x=left)),
-            send(PB.at[k, opp, high], g1.at[k, 1], dev(x=right)),
+            send(PB.at[k, 3, low], g1.at[k, 0], dev(x=left)),
+            send(PB.at[k, 3, high], g1.at[k, 1], dev(x=right)),
         ]
-        term(left)
-        b2 = [send(PB.at[k, left, high], g2.at[k, 0, high], dev(x=left))]
-        term(right)
-        b2.append(send(PB.at[k, right, low], g2.at[k, 1, low], dev(x=right)))
-        term(x)
-        yield
-        arrive(a)
-        gs[k, 0] = (PB[k, left, low].astype(F32) + g1[k, 0].astype(F32)).astype(BF16)
+        yield
+        arrive(d)
+        d = [send(DL.at[k, c, near], DL.at[k, c, near], dev(c=oc))]
+        yield
+        arrive(d)
+        term(1)
+        b2 = [send(PB.at[k, 1, high], g2.at[k, 0, high], dev(x=left))]
+        term(2)
+        b2.append(send(PB.at[k, 2, low], g2.at[k, 1, low], dev(x=right)))
+        term(0)
+        yield
+        arrive(a)
+        gs[k, 0] = (PB[k, 1, low].astype(F32) + g1[k, 0].astype(F32)).astype(BF16)
         b2.append(send(gs.at[k, 0], g2.at[k, 0, low], dev(x=left)))
-        gs[k, 1] = (PB[k, right, high].astype(F32) + g1[k, 1].astype(F32)).astype(BF16)
+        gs[k, 1] = (PB[k, 2, high].astype(F32) + g1[k, 1].astype(F32)).astype(BF16)
         b2.append(send(gs.at[k, 1], g2.at[k, 1, high], dev(x=right)))
-        if last:
-            h_all = HH[...].reshape(nc * NX * ny * ROWS, dw)
-            for i in range(2):
-                d_all = DL[:, i].reshape(nc * NX * ny * ROWS, vh)
-                t = lax.dot_general(
-                    d_all, h_all, (((0,), (0,)), ((), ())), preferred_element_type=F32
-                )
-                head_ref[i * vh : (i + 1) * vh, :] = t.astype(BF16)
         yield
         arrive(b2)
         for t in ys + [y]:
-            q = PB[k, x, t].astype(F32) + g2[k, 0, t].astype(F32) + g2[k, 1, t].astype(F32)
+            q = PB[k, 0, t].astype(F32) + g2[k, 0, t].astype(F32) + g2[k, 1, t].astype(F32)
             qf[k, t] = q
             qs[k, t] = q.astype(BF16)
         a = [send(qs.at[k, t], qr.at[k, y], dev(y=t)) for t in ys]
@@ -327,12 +329,23 @@
                 loss = loss + lossz[i]
             loss_ref[0, 0] = jnp.max(loss[0:1]) * (-1.0 / (n_own * NX * ny))
 
-    plan = [(t, -1) for t in (0.0,) + NORM_READY]
-    plan += [(t + STAGGER * k, k) for k in range(nc) for t in READY]
-    runs = {-1: norm()}
+    def gather():
+        for k in range(1, nc):
+            gather_y(k)
+            yield
+
+    def head():
+        h_all = HH[...].reshape(nc * NX * ny * ROWS, dw)
+        for i in range(2):
+            d_all = DL[:, i].reshape(nc * NX * ny * ROWS, vh)
+            t = lax.dot_general(d_all, h_all, (((0,), (0,)), ((), ())), preferred_element_type=F32)
+            head_ref[i * vh : (i + 1) * vh, :] = t.astype(BF16)
+        yield
+
+    runs = {NORM: norm(), GATHER: gather(), HEAD: head()}
     runs.update((k, chunk(k)) for k in range(nc))
-    for _, k in sorted(plan):
-        next(runs[k], None)
+    for step in PLAN:
+        next(runs[step], None)
     for cp in started:
         cp.wait_send()
 
@@ -346,7 +359,7 @@
     nc = n_own // ROWS
     vh = vl // 2
 
-    per_chunk = 4 * (ny - 1) + 3 * (nz - 1) + 2 + 2 + NX + 1 + (NX - 1) + 1 + 6
+    per_chunk = 3 * (ny - 1) + 4 * (nz - 1) + 2 + 2 + NX + 1 + (NX - 1) + 2 + 6
     n_sends = 1 + (nz - 1) + (ny - 1) + (NX - 1) + nc * per_chunk + nz - 1
     any_space = pl.BlockSpec(memory_space=pl.ANY)
     vm = pl.BlockSpec(memory_space=pltpu.VMEM)
@@ -386,6 +399,7 @@
             pltpu.VMEM((nc, 2) + tile, F32),
             pltpu.VMEM((nc, ny) + tile, F32),
             pltpu.VMEM((nc, NX) + tile, F32),
+            pltpu.VMEM((nc, NX, ROWS, vh), BF16),
             pltpu.VMEM((nc, 2, NX, ny, ROWS, vh), BF16),
             pltpu.VMEM((nc, NX, ny, ROWS, dw), BF16),
             pltpu.VMEM((nc, 2, ny // 2, ROWS, dw), BF16),

time: 107 us -> 99.6 us (0.931)
  Pallas kernels: 102 us -> 94.3 us
    pallas_call x1, Pallas kernels: 102 us -> 94.3 us  [per_device(): pl.pallas_call(functools.partial(kernel, ny, nz, nc), out_shape=(jax.Shap...]
where the time goes in v3:
time: 99.6 us; the launch traced here: 99.5 us
  Pallas kernels  94.3 us (95%)
  local copies, waits for them, and re-layouts  2.76 us (3%)
  between operations  2.42 us (2%)
    pallas_call x1, Pallas kernels, per_device(): pl.pallas_call(functools.partial(kernel, ny, nz, nc), out_shape=(jax.Shap...  94.3 us
    unnamed x4, local copies, waits for them, and re-layouts  2.76 us

profile of v3, /device:TPU:1, one launch (start us, length us, event | category | flops | bytes accessed | tf_op | source)
XLA Modules:
  0.0 99.5 jit_solution(17092727271232573157)
XLA Ops:
  0.6 94.3 %shard_map.103 = (f32[1,1]{1,0:T(1,128)}, bf16[512,768]{1,0:T(8,128)(2,1)}, f32[48,768]{1,0:T(8,128)}) custom-call(bf16[48,768]{1,0:T(8,128)(2,1)} %res_hbm.1, f32[768]{0:T(1024)} %gain_hbm.1, bf16[512,768]{1,0:T(8,128)(2,1)} %w_hbm.1, s32[1536]{0:T(1024)} %act_hbm.1, f32[1536]{0:T(1024)} %beh_hbm.1, f32[1536]{0:T(1024)} %adv_hbm.1, s32[1536]{0:T(1024)} %mask_hbm.1, ...), custom_call_target="tpu_custom_call" | custom-call | tf_op jit(solution)/shard_map/pallas_call | solution.py:367
  95.6 0.0 copy-start
  95.6 2.1 %copy.15 = bf16[512,768]{1,0:T(8,128)(2,1)} copy(bf16[512,768]{1,0:T(8,128)(2,1)} %get-tuple-element.13) | data formatting | bytes 1572864
  97.7 0.0 copy-done
  97.7 0.7 copy.16
Async XLA Ops:
  95.6 2.1 %copy-start = (f32[48,768]{1,0:T(8,128)S(1)}, f32[48,768]{1,0:T(8,128)}, u32[]{:S(2)}) copy-start(f32[48,768]{1,0:T(8,128)} %get-tuple-element.14) | copy-start | bytes 442372

commit v4 on v3

--- a/solution.py
+++ b/solution.py
@@ -13,9 +13,9 @@
 ROWS = 16
 NORM, GATHER, HEAD = -1, 3, 4
 PLAN = (
-    -1, -1, 0, -1, 3, 3, -1, 0, 1, -1, 0, 2, 0, 0, 1, 1, 0, 1, 2, 2, 1, 0, 1, 0,
-    2, 2, 2, 1, 0, 1, 0, 2, 1, 2, 0, 0, 1, 0, 2, 0, 0, 1, 2, 1, 1, 1, 2, 0,
-    2, 1, 2, 2, 2, 0, 1, 2, 4, 1, 2,
+    -1, -1, 0, -1, 3, 3, -1, 0, 1, -1, 0, 0, 0, 1, 2, 0, 1, 1, 1, 0, 1, 0, 2, 2,
+    2, 1, 0, 1, 2, 2, 0, 1, 2, 2, 0, 1, 0, 0, 2, 0, 1, 1, 2, 0, 1, 1, 2, 1,
+    2, 0, 2, 2, 1, 2, 4, 2, 0, 2, 1, 2,
 )
 FAR_FIRST = (4, 3, 5, 2, 6, 1, 7)
 LANES = 128
@@ -210,10 +210,9 @@
         arrive(b)
         near = pl.ds(0, NX - 1)
         b = []
-        for t in zs + [z]:
+        for t in zs:
             for pos in range(NX - 1):
                 cs[k, t, pos] = (Lo[k, pos, t] + xr[k, pos, t].astype(F32)).astype(BF16)
-        for t in zs:
             b.append(send(cs.at[k, t, near], cr.at[k, z, near], dev(z=t)))
         yield
         arrive(a)
@@ -305,17 +304,26 @@
         term(0)
         yield
         arrive(a)
-        gs[k, 0] = (PB[k, 1, low].astype(F32) + g1[k, 0].astype(F32)).astype(BF16)
-        b2.append(send(gs.at[k, 0], g2.at[k, 0, low], dev(x=left)))
-        gs[k, 1] = (PB[k, 2, high].astype(F32) + g1[k, 1].astype(F32)).astype(BF16)
-        b2.append(send(gs.at[k, 1], g2.at[k, 1, high], dev(x=right)))
-        yield
-        arrive(b2)
-        for t in ys + [y]:
-            q = PB[k, 0, t].astype(F32) + g2[k, 0, t].astype(F32) + g2[k, 1, t].astype(F32)
-            qf[k, t] = q
-            qs[k, t] = q.astype(BF16)
-        a = [send(qs.at[k, t], qr.at[k, y], dev(y=t)) for t in ys]
+        parts = [pl.ds(i * (dw // 2), dw // 2) for i in range(2)] if last else [pl.ds(0, dw)]
+        sums = []
+        for p in parts:
+            gs[k, 0, :, :, p] = (PB[k, 1, low, :, p].astype(F32) + g1[k, 0, :, :, p].astype(F32)).astype(BF16)
+            sums.append([send(gs.at[k, 0, :, :, p], g2.at[k, 0, low, :, p], dev(x=left))])
+            gs[k, 1, :, :, p] = (PB[k, 2, high, :, p].astype(F32) + g1[k, 1, :, :, p].astype(F32)).astype(BF16)
+            sums[-1].append(send(gs.at[k, 1, :, :, p], g2.at[k, 1, high, :, p], dev(x=right)))
+        a = []
+        for i, p in enumerate(parts):
+            yield
+            arrive(sums[i])
+            if i == 0:
+                arrive(b2)
+            for t in ys + [y]:
+                q = PB[k, 0, t, :, p].astype(F32)
+                q = q + g2[k, 0, t, :, p].astype(F32) + g2[k, 1, t, :, p].astype(F32)
+                qf[k, t, :, p] = q
+                qs[k, t, :, p] = q.astype(BF16)
+                if t is not y:
+                    a.append(send(qs.at[k, t, :, p], qr.at[k, y, :, p], dev(y=t)))
         yield
         arrive(a)
         q = qf[k, y]
@@ -360,7 +368,7 @@
     vh = vl // 2
 
     per_chunk = 3 * (ny - 1) + 4 * (nz - 1) + 2 + 2 + NX + 1 + (NX - 1) + 2 + 6
-    n_sends = 1 + (nz - 1) + (ny - 1) + (NX - 1) + nc * per_chunk + nz - 1
+    n_sends = 1 + (nz - 1) + (ny - 1) + (NX - 1) + nc * per_chunk + nz - 1 + 2 + (ny - 1)
     any_space = pl.BlockSpec(memory_space=pl.ANY)
     vm = pl.BlockSpec(memory_space=pltpu.VMEM)
     tile = (8, LANES)

time: 99.6 us -> 97.5 us (0.979)
  Pallas kernels: 94.3 us -> 91.9 us
    pallas_call x1, Pallas kernels: 94.3 us -> 91.9 us  [per_device(): pl.pallas_call(functools.partial(kernel, ny, nz, nc), out_shape=(jax.Shap...]
where the time goes in v4:
time: 97.5 us; the launch traced here: 97.1 us
  Pallas kernels  91.9 us (94%)
  local copies, waits for them, and re-layouts  2.76 us (3%)
  between operations  2.42 us (2%)
    pallas_call x1, Pallas kernels, per_device(): pl.pallas_call(functools.partial(kernel, ny, nz, nc), out_shape=(jax.Shap...  91.9 us
    unnamed x4, local copies, waits for them, and re-layouts  2.76 us

profile of v4, /device:TPU:1, one launch (start us, length us, event | category | flops | bytes accessed | tf_op | source)
XLA Modules:
  0.0 97.1 jit_solution(18071601244175856086)
XLA Ops:
  0.6 91.9 %shard_map.103 = (f32[1,1]{1,0:T(1,128)}, bf16[512,768]{1,0:T(8,128)(2,1)}, f32[48,768]{1,0:T(8,128)}) custom-call(bf16[48,768]{1,0:T(8,128)(2,1)} %res_hbm.1, f32[768]{0:T(1024)} %gain_hbm.1, bf16[512,768]{1,0:T(8,128)(2,1)} %w_hbm.1, s32[1536]{0:T(1024)} %act_hbm.1, f32[1536]{0:T(1024)} %beh_hbm.1, f32[1536]{0:T(1024)} %adv_hbm.1, s32[1536]{0:T(1024)} %mask_hbm.1, ...), custom_call_target="tpu_custom_call" | custom-call | tf_op jit(solution)/shard_map/pallas_call | solution.py:375
  93.2 0.0 copy-start
  93.2 2.1 %copy.15 = bf16[512,768]{1,0:T(8,128)(2,1)} copy(bf16[512,768]{1,0:T(8,128)(2,1)} %get-tuple-element.13) | data formatting | bytes 1572864
  95.3 0.0 copy-done
  95.3 0.7 copy.16
Async XLA Ops:
  93.2 2.1 %copy-start = (f32[48,768]{1,0:T(8,128)S(1)}, f32[48,768]{1,0:T(8,128)}, u32[]{:S(2)}) copy-start(f32[48,768]{1,0:T(8,128)} %get-tuple-element.14) | copy-start | bytes 442372

commit v5 on v4

--- a/solution.py
+++ b/solution.py
@@ -13,10 +13,11 @@
 ROWS = 16
 NORM, GATHER, HEAD = -1, 3, 4
 PLAN = (
-    -1, -1, 0, -1, 3, 3, -1, 0, 1, -1, 0, 0, 0, 1, 2, 0, 1, 1, 1, 0, 1, 0, 2, 2,
-    2, 1, 0, 1, 2, 2, 0, 1, 2, 2, 0, 1, 0, 0, 2, 0, 1, 1, 2, 0, 1, 1, 2, 1,
-    2, 0, 2, 2, 1, 2, 4, 2, 0, 2, 1, 2,
+    -1, 3, -1, 0, -1, 3, 1, 0, -1, 0, 0, 1, 2, 0, -1, 0, 1, 1, 1, 0, 1, 2, 0, 2,
+    2, 2, 0, 1, 2, 1, 0, 2, 1, 2, 0, 0, 1, 0, 2, 0, 0, 1, 2, 1, 1, 1, 1, 2,
+    2, 2, 0, 2, 1, 2, 2, 2, 1, 0, 4, 2,
 )
+RAW = 0
 FAR_FIRST = (4, 3, 5, 2, 6, 1, 7)
 LANES = 128
 F32 = jnp.float32
@@ -82,6 +83,14 @@
     zs = [lax.rem(z + d, nz) for d in FAR_FIRST if d < nz]
     others = [opp, right, left]
 
+    barrier = pltpu.get_barrier_semaphore()
+    partners = (
+        [dev(y=t) for t in ys[:3]] + [dev(z=t) for t in zs] + [dev(y=t) for t in ys[3:]]
+        + [dev(x=t) for t in others] + [dev(c=oc)]
+    )
+    for p in partners:
+        pl.semaphore_signal(barrier, inc=1, device_id=p, device_id_type=pl.DeviceIdType.MESH)
+
     loads = []
     pairs = ((res_hbm, res), (gain_hbm, gain), (w_hbm, w), (act_hbm, act), (beh_hbm, beh),
              (adv_hbm, adv), (mask_hbm, mask), (clip_hbm, clip))
@@ -104,13 +113,6 @@
     def arrive(copies):
         for cp in copies:
             cp.wait_recv()
-
-    barrier = pltpu.get_barrier_semaphore()
-    partners = (
-        [dev(y=t) for t in ys] + [dev(z=t) for t in zs] + [dev(x=t) for t in others] + [dev(c=oc)]
-    )
-    for p in partners:
-        pl.semaphore_signal(barrier, inc=1, device_id=p, device_id_type=pl.DeviceIdType.MESH)
 
     loads[0].wait()
     sq = res[...].astype(F32)
@@ -177,12 +179,29 @@
             out = jnp.where((lane >= i * ROWS) & (lane < (i + 1) * ROWS), t, out)
         return out
 
-    def terms(k, pos):
+    def own_inv(k):
+        out = jnp.zeros((1, LANES), F32)
+        for i in range(NX):
+            t = jnp.broadcast_to(inx[i, pl.ds(z, 1)], (8, LANES))
+            shift = (LANES + (i - k) * ROWS) % LANES
+            t = (pltpu.roll(t, shift, 1) if shift else t)[0:1]
+            out = jnp.where((lane[0:1] >= i * ROWS) & (lane[0:1] < (i + 1) * ROWS), t, out)
+        return out
+
+    def normed(k, pos):
         at = order[pos]
         cols = invc[at]
         for j in range(ny):
             unit = H[k, at, j].astype(F32) * cols[k * ROWS : (k + 1) * ROWS, j : j + 1]
             HH[k, pos, j] = (unit * gain[...].reshape(1, dw)).astype(BF16)
+
+    def terms(k, pos):
+        at = order[pos]
+        if k == RAW:
+            for j in range(ny):
+                HH[k, pos, j] = (H[k, at, j].astype(F32) * gain[...].reshape(1, dw)).astype(BF16)
+        else:
+            normed(k, pos)
         h = HH[k, pos].reshape(ny * ROWS, dw)
         w_other = w[pl.ds(pl.multiple_of(oc * vh, vh), vh)]
         t = lax.dot_general(h, w_other, (((1,), (1,)), ((), ())), preferred_element_type=F32)
@@ -231,6 +250,9 @@
                 logits = logits + cr[k, t, pos].astype(F32)
             lg[k, order[pos]] = logits
         logits = lg[k].reshape(tp, vh)
+        if k == RAW:
+            logits = logits * as_columns(stack_rows(own_inv(k)), tp)[:, 0:1]
+            lg[k] = logits.reshape(NX, ROWS, vh)
 
         tok = own_tokens(k)
         column = lax.broadcasted_iota(jnp.int32, (tp, vh), 1).astype(F32)
@@ -324,6 +346,9 @@
                 qs[k, t, :, p] = q.astype(BF16)
                 if t is not y:
                     a.append(send(qs.at[k, t, :, p], qr.at[k, y, :, p], dev(y=t)))
+        if k == RAW:
+            for pos in range(NX):
+                normed(k, pos)
         yield
         arrive(a)
         q = qf[k, y]

time: 97.5 us -> 98.5 us (1.010)
  Pallas kernels: 91.9 us -> 93.1 us
    pallas_call x1, Pallas kernels: 91.9 us -> 93.1 us  [per_device(): pl.pallas_call(functools.partial(kernel, ny, nz, nc), out_shape=(jax.Shap...]
where the time goes in v5:
time: 98.5 us; the launch traced here: 98.3 us
  Pallas kernels  93.1 us (95%)
  local copies, waits for them, and re-layouts  2.76 us (3%)
  between operations  2.42 us (2%)
    pallas_call x1, Pallas kernels, per_device(): pl.pallas_call(functools.partial(kernel, ny, nz, nc), out_shape=(jax.Shap...  93.1 us
    unnamed x4, local copies, waits for them, and re-layouts  2.76 us

profile of v5, /device:TPU:1, one launch (start us, length us, event | category | flops | bytes accessed | tf_op | source)
XLA Modules:
  0.0 98.3 jit_solution(5881795383730585137)
XLA Ops:
  0.6 93.1 %shard_map.103 = (f32[1,1]{1,0:T(1,128)}, bf16[512,768]{1,0:T(8,128)(2,1)}, f32[48,768]{1,0:T(8,128)}) custom-call(bf16[48,768]{1,0:T(8,128)(2,1)} %res_hbm.1, f32[768]{0:T(1024)} %gain_hbm.1, bf16[512,768]{1,0:T(8,128)(2,1)} %w_hbm.1, s32[1536]{0:T(1024)} %act_hbm.1, f32[1536]{0:T(1024)} %beh_hbm.1, f32[1536]{0:T(1024)} %adv_hbm.1, s32[1536]{0:T(1024)} %mask_hbm.1, ...), custom_call_target="tpu_custom_call" | custom-call | tf_op jit(solution)/shard_map/pallas_call | solution.py:400
  94.4 0.0 copy-start
  94.4 2.1 %copy.15 = bf16[512,768]{1,0:T(8,128)(2,1)} copy(bf16[512,768]{1,0:T(8,128)(2,1)} %get-tuple-element.13) | data formatting | bytes 1572864
  96.5 0.0 copy-done
  96.5 0.7 copy.16
Async XLA Ops:
  94.4 2.1 %copy-start = (f32[48,768]{1,0:T(8,128)S(1)}, f32[48,768]{1,0:T(8,128)}, u32[]{:S(2)}) copy-start(f32[48,768]{1,0:T(8,128)} %get-tuple-element.14) | copy-start | bytes 442372

commit v6 on v4

--- a/solution.py
+++ b/solution.py
@@ -58,8 +58,8 @@
 def kernel(
     ny, nz, nc,
     res_hbm, gain_hbm, w_hbm, act_hbm, beh_hbm, adv_hbm, mask_hbm, clip_hbm,
-    loss_ref, head_ref, hid_ref,
-    res, gain, w, act, beh, adv, mask, clip, tk,
+    loss_ref, head_hbm, hid_ref,
+    head_ref, res, gain, w, act, beh, adv, mask, clip, tk,
     sqc, sqz, iny, inx, invc, H, HH, Lo, xs, xr, cs, cr, lg, dcb, dyb, dxb, dlx, DL, PB,
     g1, g2, gs, qf, qs, qr, lossz, lsem, ssem, rsem,
 ):
@@ -82,6 +82,13 @@
     zs = [lax.rem(z + d, nz) for d in FAR_FIRST if d < nz]
     others = [opp, right, left]
 
+    barrier = pltpu.get_barrier_semaphore()
+    partners = (
+        [dev(y=t) for t in ys] + [dev(z=t) for t in zs] + [dev(x=t) for t in others] + [dev(c=oc)]
+    )
+    for p in partners:
+        pl.semaphore_signal(barrier, inc=1, device_id=p, device_id_type=pl.DeviceIdType.MESH)
+
     loads = []
     pairs = ((res_hbm, res), (gain_hbm, gain), (w_hbm, w), (act_hbm, act), (beh_hbm, beh),
              (adv_hbm, adv), (mask_hbm, mask), (clip_hbm, clip))
@@ -104,13 +111,6 @@
     def arrive(copies):
         for cp in copies:
             cp.wait_recv()
-
-    barrier = pltpu.get_barrier_semaphore()
-    partners = (
-        [dev(y=t) for t in ys] + [dev(z=t) for t in zs] + [dev(x=t) for t in others] + [dev(c=oc)]
-    )
-    for p in partners:
-        pl.semaphore_signal(barrier, inc=1, device_id=p, device_id_type=pl.DeviceIdType.MESH)
 
     loads[0].wait()
     sq = res[...].astype(F32)
@@ -342,12 +342,17 @@
             gather_y(k)
             yield
 
+    stores = []
+
     def head():
         h_all = HH[...].reshape(nc * NX * ny * ROWS, dw)
         for i in range(2):
             d_all = DL[:, i].reshape(nc * NX * ny * ROWS, vh)
             t = lax.dot_general(d_all, h_all, (((0,), (0,)), ((), ())), preferred_element_type=F32)
-            head_ref[i * vh : (i + 1) * vh, :] = t.astype(BF16)
+            rows = pl.ds(i * vh, vh)
+            head_ref[rows, :] = t.astype(BF16)
+            stores.append(pltpu.make_async_copy(head_ref.at[rows], head_hbm.at[rows], lsem.at[8 + i]))
+            stores[-1].start()
         yield
 
     runs = {NORM: norm(), GATHER: gather(), HEAD: head()}
@@ -356,6 +361,8 @@
         next(runs[step], None)
     for cp in started:
         cp.wait_send()
+    for cp in stores:
+        cp.wait()
 
 
 def per_device(mesh_sizes, residual, norm_gain, head_weight, actions, behavior_logp, advantages, decision_mask, clip_tenths):
@@ -380,8 +387,9 @@
             jax.ShapeDtypeStruct((n_own, dw), F32),
         ),
         in_specs=[any_space] * 8,
-        out_specs=(pl.BlockSpec(memory_space=pltpu.SMEM), vm, vm),
+        out_specs=(pl.BlockSpec(memory_space=pltpu.SMEM), any_space, vm),
         scratch_shapes=[
+            pltpu.VMEM((vl, dw), BF16),
             pltpu.VMEM((n_own, dw), BF16),
             pltpu.VMEM((dw,), F32),
             pltpu.VMEM((vl, dw), BF16),
@@ -417,7 +425,7 @@
             pltpu.VMEM((nc, ny, ROWS, dw), BF16),
             pltpu.VMEM((nc, ny, ROWS, dw), BF16),
             pltpu.VMEM((nz,) + tile, F32),
-            pltpu.SemaphoreType.DMA((8,)),
+            pltpu.SemaphoreType.DMA((10,)),
             pltpu.SemaphoreType.DMA((n_sends,)),
             pltpu.SemaphoreType.DMA((n_sends,)),
         ],

time: 97.5 us -> 97.4 us (level)
  no operation moved by 1% of the time
where the time goes in v6:
time: 97.4 us; the launch traced here: 97.2 us
  Pallas kernels  92.1 us (95%)
  local copies, waits for them, and re-layouts  2.76 us (3%)
  between operations  2.42 us (2%)
    pallas_call x1, Pallas kernels, per_device(): pl.pallas_call(functools.partial(kernel, ny, nz, nc), out_shape=(jax.Shap...  92.1 us
    unnamed x4, local copies, waits for them, and re-layouts  2.76 us

profile of v6, /device:TPU:1, one launch (start us, length us, event | category | flops | bytes accessed | tf_op | source)
XLA Modules:
  0.0 97.2 jit_solution(14794958041124056029)
XLA Ops:
  0.6 92.1 %shard_map.103 = (f32[1,1]{1,0:T(1,128)}, bf16[512,768]{1,0:T(8,128)(2,1)}, f32[48,768]{1,0:T(8,128)}) custom-call(bf16[48,768]{1,0:T(8,128)(2,1)} %res_hbm.1, f32[768]{0:T(1024)} %gain_hbm.1, bf16[512,768]{1,0:T(8,128)(2,1)} %w_hbm.1, s32[1536]{0:T(1024)} %act_hbm.1, f32[1536]{0:T(1024)} %beh_hbm.1, f32[1536]{0:T(1024)} %adv_hbm.1, s32[1536]{0:T(1024)} %mask_hbm.1, ...), custom_call_target="tpu_custom_call" | custom-call | tf_op jit(solution)/shard_map/pallas_call | solution.py:382
  93.3 0.0 copy-start
  93.3 2.1 %copy.15 = bf16[512,768]{1,0:T(8,128)(2,1)} copy(bf16[512,768]{1,0:T(8,128)(2,1)} %get-tuple-element.13) | data formatting | bytes 1572864
  95.5 0.0 copy-done
  95.5 0.7 copy.16
Async XLA Ops:
  93.3 2.1 %copy-start = (f32[48,768]{1,0:T(8,128)S(1)}, f32[48,768]{1,0:T(8,128)}, u32[]{:S(2)}) copy-start(f32[48,768]{1,0:T(8,128)} %get-tuple-element.14) | copy-start | bytes 442372

commit v7 on v6

--- a/solution.py
+++ b/solution.py
@@ -196,15 +196,17 @@
     def chunk(k):
         last = k == nc - 1
         arrive(gathers[k])
-        a = [send(H.at[k, x], H.at[k, x], dev(x=t)) for t in (right, left)]
-        yield
-        arrive(a)
         low, high = pl.ds(0, half), pl.ds(half, half)
+        a = [send(H.at[k, x, p], H.at[k, x, p], dev(x=t)) for t, p in ((right, low), (left, high))]
+        b = [send(H.at[k, x, p], H.at[k, x, p], dev(x=t)) for t, p in ((right, high), (left, low))]
+        yield
+        arrive(a)
         a = [
             send(H.at[k, left, low], H.at[k, left, low], dev(x=right)),
             send(H.at[k, right, high], H.at[k, right, high], dev(x=left)),
         ]
         yield
+        arrive(b)
         b = [terms(k, pos) for pos in range(NX - 1)]
         yield
         arrive(b)
@@ -374,7 +376,7 @@
     nc = n_own // ROWS
     vh = vl // 2
 
-    per_chunk = 3 * (ny - 1) + 4 * (nz - 1) + 2 + 2 + NX + 1 + (NX - 1) + 2 + 6
+    per_chunk = 3 * (ny - 1) + 4 * (nz - 1) + 4 + 2 + NX + 1 + (NX - 1) + 2 + 6
     n_sends = 1 + (nz - 1) + (ny - 1) + (NX - 1) + nc * per_chunk + nz - 1 + 2 + (ny - 1)
     any_space = pl.BlockSpec(memory_space=pl.ANY)
     vm = pl.BlockSpec(memory_space=pltpu.VMEM)

time: 97.4 us -> 98 us (level)
  no operation moved by 1% of the time
where the time goes in v7:
time: 98 us; the launch traced here: 97.8 us
  Pallas kernels  92.6 us (94%)
  local copies, waits for them, and re-layouts  2.76 us (3%)
  between operations  2.42 us (2%)
    pallas_call x1, Pallas kernels, per_device(): pl.pallas_call(functools.partial(kernel, ny, nz, nc), out_shape=(jax.Shap...  92.6 us
    unnamed x4, local copies, waits for them, and re-layouts  2.76 us

profile of v7, /device:TPU:1, one launch (start us, length us, event | category | flops | bytes accessed | tf_op | source)
XLA Modules:
  0.0 97.8 jit_solution(9029764900289326543)
XLA Ops:
  0.6 92.6 %shard_map.103 = (f32[1,1]{1,0:T(1,128)}, bf16[512,768]{1,0:T(8,128)(2,1)}, f32[48,768]{1,0:T(8,128)}) custom-call(bf16[48,768]{1,0:T(8,128)(2,1)} %res_hbm.1, f32[768]{0:T(1024)} %gain_hbm.1, bf16[512,768]{1,0:T(8,128)(2,1)} %w_hbm.1, s32[1536]{0:T(1024)} %act_hbm.1, f32[1536]{0:T(1024)} %beh_hbm.1, f32[1536]{0:T(1024)} %adv_hbm.1, s32[1536]{0:T(1024)} %mask_hbm.1, ...), custom_call_target="tpu_custom_call" | custom-call | tf_op jit(solution)/shard_map/pallas_call | solution.py:384
  93.9 0.0 copy-start
  93.9 2.1 %copy.15 = bf16[512,768]{1,0:T(8,128)(2,1)} copy(bf16[512,768]{1,0:T(8,128)(2,1)} %get-tuple-element.13) | data formatting | bytes 1572864
  96.0 0.0 copy-done
  96.0 0.7 copy.16
Async XLA Ops:
  93.9 2.1 %copy-start = (f32[48,768]{1,0:T(8,128)S(1)}, f32[48,768]{1,0:T(8,128)}, u32[]{:S(2)}) copy-start(f32[48,768]{1,0:T(8,128)} %get-tuple-element.14) | copy-start | bytes 442372
